TPU v7x, 512 devices: a whole 4x4x16 slice. The times are simulated.
512 devices in a mesh: row: 16 (over x, y), col: 16 (over z_lo, core), depth: 2 (over z_hi).
Axes of the slice: x: 4, y: 4, z: 16 (z_hi: 2, z_lo: 8; z = z_hi * 8 + z_lo), core: 2. Of those that a mesh axis runs over, the one named last changes fastest.
Arguments:
- grad_out: bfloat16 [65536, 512], P(('row', 'col', 'depth')), may hold values from -6 to 6
- relu_mask: int32 [65536, 512], P(('row', 'col', 'depth')), may hold values 0 or 1
- aggregated: bfloat16 [65536, 512], P(('row', 'col', 'depth')), may hold values from -0.0234375 to 0.0234375
- weight: bfloat16 [512, 512], replicated, may hold values from -0.25 to 0.25
- adjacency_tiles: bfloat16 [43008, 128, 128], P(('row', 'col', 'depth')), may hold values from -0.09375 to 0.09375
- tile_rows: int32 [43008], P(('row', 'col', 'depth')), may hold values from 0 to 15
- tile_cols: int32 [43008], P(('row', 'col', 'depth')), may hold values from 0 to 31
- tile_count: int32 [512], P(('row', 'col', 'depth')), may hold values from 10 to 84, as said below
Outputs:
- node_grad: bfloat16 [65536, 512], P(('row', 'col', 'depth'))
- weight_grad: float32 [512, 512], replicated
Inputs may be any that keep to these rules, and one draw needn't show every extreme that they name: `tile_count`: some device has all 84 slots live in every draw; most have far fewer.
All inputs are finite; a program needn't handle non-finite values. No bound on the sum of `relu_mask` on one device may be relied on, other than what follows from the above.
Results may differ from a plain program's by a relative error of at most 0.024.
Values may be sent and summed in bfloat16 or wider, within the bound.
A program may use at most 64 MiB of HBM per device.

v0:
```python
import jax
import jax.numpy as jnp
from jax import lax
from jax.sharding import PartitionSpec as P


def on_device(
    grad_out, relu_mask, aggregated, weight, adjacency_tiles, tile_rows, tile_cols, tile_count
):
    rows_dev = grad_out.shape[0]
    feature_count = grad_out.shape[1]
    slot_count = adjacency_tiles.shape[0]
    tile_size = adjacency_tiles.shape[1]
    grad_pre = grad_out * relu_mask.astype(jnp.bfloat16)
    local_grad = lax.dot_general(
        aggregated, grad_pre, (((0,), (0,)), ((), ())), preferred_element_type=jnp.float32
    )
    projected = lax.dot_general(
        grad_pre, weight, (((1,), (1,)), ((), ())), preferred_element_type=jnp.float32
    )
    projected = projected.astype(jnp.bfloat16)
    gathered = lax.all_gather(projected, "col", axis=0, tiled=True)
    slab_panel = gathered.reshape(-1, tile_size, feature_count)
    group_count = lax.axis_size("row") * lax.axis_size("depth") * rows_dev // tile_size
    live_count = tile_count[0]
    block_size = 1
    for candidate in range(min(12, slot_count), 0, -1):
        block_size = candidate
        break

    def add_block(step_index, partial_value):
        offset = step_index * block_size
        picked_tiles = lax.dynamic_slice_in_dim(adjacency_tiles, offset, block_size, 0)
        row_index = lax.dynamic_slice_in_dim(tile_rows, offset, block_size, 0)
        col_index = lax.dynamic_slice_in_dim(tile_cols, offset, block_size, 0)
        alive_mask = (offset + jnp.arange(block_size) < live_count).astype(jnp.bfloat16)
        picked_tiles = picked_tiles * alive_mask[:, None, None]
        picked_rows = slab_panel[row_index]
        products = jnp.einsum(
            "kab,kaf->kbf", picked_tiles, picked_rows, preferred_element_type=jnp.float32
        )
        return partial_value.at[col_index].add(products)

    start_partial = jnp.zeros((group_count, tile_size, feature_count), jnp.float32)
    partial_value = lax.fori_loop(0, slot_count // block_size, add_block, start_partial)
    summed = lax.psum_scatter(
        partial_value.reshape(group_count * tile_size, feature_count).astype(jnp.bfloat16),
        ("row", "depth"),
        scatter_dimension=0,
        tiled=True,
    )
    weight_grad = lax.psum(local_grad, ("row", "col", "depth"))
    return (summed, weight_grad)


def solution(mesh):
    return jax.shard_map(
        on_device,
        mesh=mesh,
        in_specs=(
            P(("row", "col", "depth"), None),
            P(("row", "col", "depth"), None),
            P(("row", "col", "depth"), None),
            P(),
            P(("row", "col", "depth"), None, None),
            P(("row", "col", "depth")),
            P(("row", "col", "depth")),
            P(("row", "col", "depth")),
        ),
        out_specs=(P(("row", "col", "depth"), None), P()),
        check_vma=False,
    )
```

profile of v0, /device:TPU:1, one launch (start us, length us, event | category | flops | bytes accessed | tf_op | source)
XLA Modules:
  0.0 684.1 jit_solution(11226902094686097739)
XLA Ops:
  9.0 2.0 convolution_convert_fusion
  11.1 2.3 convolution_bitcast_fusion
  13.5 104.9 %all-gather.2.cloned.1.call-done = bf16[2048,512]{1,0:T(8,128)(2,1)} async-done(((bf16[128,512]{1,0:T(8,128)(2,1)}), bf16[2048,512]{1,0:T(8,128)(2,1)}) %all-gather.2.cloned.1.call-update) | async-done | bytes 2097168 | tf_op jit(solution)/shard_map/all_gather | solution.py:22
  118.4 4.3 broadcast_in_dim.20
  122.7 108.1 %while.13 = (s32[]{:T(128)}, f32[32,128,512]{2,1,0:T(8,128)}, s32[84]{0:T(128)S(1)}, bf16[84,128,128]{2,1,0:T(8,128)(2,1)}, s32[]{:T(128)}, /*index=5*/s32[84]{0...) while((s32[]{:T(128)}, f32[32,128,512]{2,1,0:T(8,128)}, ...), condition=%wide.region_2.0_spmd, body=%wide.region_0.0_spmd.sunk | while | flops 202310768 | bytes 19272236 | solution.py:45
  122.8 2.3 gather_fusion
  125.0 1.0 constant_dynamic-slice_fusion.2
  127.0 2.3 fusion.11
  129.3 8.7 %scatter_fusion = f32[32,128,512]{2,1,0:T(8,128)} fusion(f32[32,128,512]{2,1,0:T(8,128)} %get-tuple-element.211, s32[12]{0:T(128)S(1)} %get-tuple-element.197, f32[12,128,512]{2,1,0:T(8,128)} %fusion.11), kind=kCustom, calls=%fused_computation.1.clone.1 | custom fusion | flops 786432 | bytes 9437232 | tf_op jit(solution)/shard_map/while/body/eval_jaxpr/scatter-add | solution.py:42
  138.1 2.2 gather_fusion
  142.3 2.3 fusion.11
  144.6 8.9 %scatter_fusion = f32[32,128,512]{2,1,0:T(8,128)} fusion(f32[32,128,512]{2,1,0:T(8,128)} %get-tuple-element.211, s32[12]{0:T(128)S(1)} %get-tuple-element.197, f32[12,128,512]{2,1,0:T(8,128)} %fusion.11), kind=kCustom, calls=%fused_computation.1.clone.1 | custom fusion | flops 786432 | bytes 9437232 | tf_op jit(solution)/shard_map/while/body/eval_jaxpr/scatter-add | solution.py:42
  153.6 2.2 gather_fusion
  155.8 1.0 constant_dynamic-slice_fusion.2
  157.8 2.3 fusion.11
  160.1 9.0 %scatter_fusion = f32[32,128,512]{2,1,0:T(8,128)} fusion(f32[32,128,512]{2,1,0:T(8,128)} %get-tuple-element.211, s32[12]{0:T(128)S(1)} %get-tuple-element.197, f32[12,128,512]{2,1,0:T(8,128)} %fusion.11), kind=kCustom, calls=%fused_computation.1.clone.1 | custom fusion | flops 786432 | bytes 9437232 | tf_op jit(solution)/shard_map/while/body/eval_jaxpr/scatter-add | solution.py:42
  169.2 2.2 gather_fusion
  173.4 2.3 fusion.11
  175.7 8.9 %scatter_fusion = f32[32,128,512]{2,1,0:T(8,128)} fusion(f32[32,128,512]{2,1,0:T(8,128)} %get-tuple-element.211, s32[12]{0:T(128)S(1)} %get-tuple-element.197, f32[12,128,512]{2,1,0:T(8,128)} %fusion.11), kind=kCustom, calls=%fused_computation.1.clone.1 | custom fusion | flops 786432 | bytes 9437232 | tf_op jit(solution)/shard_map/while/body/eval_jaxpr/scatter-add | solution.py:42
  184.6 2.2 gather_fusion
  186.9 1.0 constant_dynamic-slice_fusion.2
  188.8 2.3 fusion.11
  191.2 8.9 %scatter_fusion = f32[32,128,512]{2,1,0:T(8,128)} fusion(f32[32,128,512]{2,1,0:T(8,128)} %get-tuple-element.211, s32[12]{0:T(128)S(1)} %get-tuple-element.197, f32[12,128,512]{2,1,0:T(8,128)} %fusion.11), kind=kCustom, calls=%fused_computation.1.clone.1 | custom fusion | flops 786432 | bytes 9437232 | tf_op jit(solution)/shard_map/while/body/eval_jaxpr/scatter-add | solution.py:42
  200.1 2.2 gather_fusion
  204.3 2.3 fusion.11
  206.6 8.9 %scatter_fusion = f32[32,128,512]{2,1,0:T(8,128)} fusion(f32[32,128,512]{2,1,0:T(8,128)} %get-tuple-element.211, s32[12]{0:T(128)S(1)} %get-tuple-element.197, f32[12,128,512]{2,1,0:T(8,128)} %fusion.11), kind=kCustom, calls=%fused_computation.1.clone.1 | custom fusion | flops 786432 | bytes 9437232 | tf_op jit(solution)/shard_map/while/body/eval_jaxpr/scatter-add | solution.py:42
  215.6 2.2 gather_fusion
  219.8 2.3 fusion.11
  222.1 8.7 %scatter_fusion = f32[32,128,512]{2,1,0:T(8,128)} fusion(f32[32,128,512]{2,1,0:T(8,128)} %get-tuple-element.211, s32[12]{0:T(128)S(1)} %get-tuple-element.197, f32[12,128,512]{2,1,0:T(8,128)} %fusion.11), kind=kCustom, calls=%fused_computation.1.clone.1 | custom fusion | flops 786432 | bytes 9437232 | tf_op jit(solution)/shard_map/while/body/eval_jaxpr/scatter-add | solution.py:42
  230.8 6.0 convert_element_type.25
  236.8 437.3 %all-reduce.2.cloned.1.call-done = f32[512,512]{0,1:T(8,128)} async-done(((f32[512,512]{0,1:T(8,128)}), f32[512,512]{0,1:T(8,128)}) %all-reduce.2.cloned.1.call-update) | async-done | bytes 1048592 | tf_op jit(solution)/shard_map/psum | solution.py:52
  674.1 2.5 copy.11
  (45 shorter events, 12.0 us)
Async XLA Ops:
  8.0 1.0 copy-start
  8.0 110.4 %all-gather.2.cloned.1.call-start = ((), (), s32[]{:S(2)}) async-start(), calls=%async_computation.1 | async-start | bytes 2228224 | tf_op jit(solution)/shard_map/all_gather | solution.py:22
  11.1 663.1 %all-reduce.2.cloned.1.call-start = ((), (), s32[]{:S(2)}) async-start(), calls=%async_computation.3 | async-start | bytes 2097152 | tf_op jit(solution)/shard_map/psum | solution.py:52
  13.5 663.2 %reduce-scatter.2.cloned.1.call-start = ((), (), s32[]{:S(2)}) async-start(), calls=%async_computation.2 | async-start | bytes 4325376 | tf_op jit(solution)/shard_map/reduce_scatter | solution.py:46
  118.4 4.3 copy-start.1
  118.4 4.3 copy-start.2
Sparse Core Ops, SparseCore 0:
  11.5 106.8 all-gather.1
  237.0 398.4 reduce-scatter.1
Sparse Core Ops, SparseCore 1:
  17.6 656.5 all-reduce.1
where the time goes:
time: 692 us; the launch traced here: 684 us
  waiting for transfers between devices  542 us (78%)
  other arithmetic  73 us (11%)
  local copies, waits for them, and re-layouts  32.3 us (5%)
  matrix products  20.7 us (3%)
  between operations  15.5 us (2%)
    psum x1, waiting for transfers between devices, on_device(): weight_grad = lax.psum(local_grad, ('row', 'col', 'depth'))  437 us
    all_gather x1, waiting for transfers between devices, on_device(): gathered = lax.all_gather(projected, 'col', axis=0, tiled=True)  105 us
    scatter-add x7, other arithmetic, add_block(): return partial_value.at[col_index].add(products)  61.9 us
    dot_general x7, matrix products, add_block(): jnp.einsum('kab,kaf->kbf', picked_tiles, picked_rows, preferred_element_t...  16.4 us
    gather x7, local copies, waits for them, and re-layouts, add_block(): picked_rows = slab_panel[row_index]  15.7 us
  transfers between devices with their start and end apart: 3, of which 2 were waited for; matrix products, arithmetic and copies ran while one was open for 18% of the time, Pallas kernels for 0%

commit v1 on v0

v1 whole, which is shorter than its diff:
```python
import jax
import jax.numpy as jnp
from jax import lax
from jax.experimental import pallas as pl
from jax.experimental.pallas import tpu as pltpu
from jax.sharding import PartitionSpec as P

MESH = pl.DeviceIdType.MESH
F32 = jnp.float32
BF16 = jnp.bfloat16
T = 128
NCHUNK = 4
SLOTS = 84
GROUP = 32
UNROLL = 6
HALF = SLOTS // 2
SEMS = 320


def wrap4(value):
    return lax.rem(value, 4)


class Ring:
    def __init__(self, k, src, unit, rl, rr, fl, fr, out, right, left):
        self.src, self.unit, self.out = src, unit, out
        self.rl, self.rr, self.fl, self.fr = rl, rr, fl, fr
        u = unit
        self.to_right = k.copy(src.at[pl.ds(3 * u, 2 * u)], rl, right)
        self.to_left = k.copy(src.at[pl.ds(5 * u, 2 * u)], rr, left)
        self.sum_right = k.copy(src.at[pl.ds(2 * u, u)], fl, right)
        self.sum_left = k.copy(src.at[pl.ds(7 * u, u)], fr, left)

    def first(self):
        self.to_right.start()
        self.to_left.start()

    def second(self):
        u, src = self.unit, self.src
        self.to_right.wait_recv()
        src[pl.ds(2 * u, u)] = (
            src[pl.ds(2 * u, u)].astype(F32) + self.rl[pl.ds(u, u)].astype(F32)
        ).astype(BF16)
        self.sum_right.start()
        self.to_left.wait_recv()
        src[pl.ds(7 * u, u)] = (
            src[pl.ds(7 * u, u)].astype(F32) + self.rr[pl.ds(0, u)].astype(F32)
        ).astype(BF16)
        self.sum_left.start()

    def last(self):
        u, src = self.unit, self.src
        self.sum_right.wait_recv()
        self.out[pl.ds(0, u)] = (
            src[pl.ds(0, u)].astype(F32)
            + self.fl[...].astype(F32)
            + self.rr[pl.ds(u, u)].astype(F32)
        ).astype(BF16)
        self.sum_left.wait_recv()
        self.out[pl.ds(u, u)] = (
            src[pl.ds(u, u)].astype(F32)
            + self.rl[pl.ds(0, u)].astype(F32)
            + self.fr[...].astype(F32)
        ).astype(BF16)


class Copies:
    def __init__(self, send_sems, recv_sems):
        self.send_sems, self.recv_sems, self.used = send_sems, recv_sems, 0
        self.all = []

    def copy(self, src, dst, device):
        index = self.used
        self.used += 1
        made = pltpu.make_async_remote_copy(
            src_ref=src,
            dst_ref=dst,
            send_sem=self.send_sems.at[index],
            recv_sem=self.recv_sems.at[index],
            device_id=device,
            device_id_type=MESH,
        )
        self.all.append(made)
        return made


def kernel(
    order_ref, gate_ref, grad_ref, mask_ref, agg_ref, weight_ref, tiles_hbm,
    node_ref, wgrad_ref,
    tiles, seg, acc_ref,
    g0, g1, g2, g3,
    parts, xl, xr, xfl, xfr, mids, yl, yr, yfl, yfr, tops, ztop,
    wl, ws, wa, wxl, wxr, wxfl, wxfr, wb, wyl, wyr, wyfl, wyfr, wc, wz, wg,
    send_sems, recv_sems, tile_sem,
):
    row, col, depth = lax.axis_index("row"), lax.axis_index("col"), lax.axis_index("depth")
    x, y = lax.div(row, 4), lax.rem(row, 4)
    z, core = lax.div(col, 2), lax.rem(col, 2)
    zz = depth * 8 + z
    gathered = (g0, g1, g2, g3)

    def device(dx=0, dy=0):
        return (wrap4(x + dx) * 4 + wrap4(y + dy), col, depth)

    def along_z(step):
        place = lax.rem(zz + step, 16)
        return (row, lax.rem(place, 8) * 2 + core, lax.div(place, 8)), place

    def along_group(step):
        place = lax.rem(z + step, 8)
        return (row, place * 2 + core, depth), place

    sibling = (row, z * 2 + 1 - core, depth)
    right_x, left_x = device(dx=1), device(dx=3)
    right_y, left_y = device(dy=1), device(dy=3)
    partner = (row, col, 1 - depth)
    k = Copies(send_sems, recv_sems)

    load_tiles = pltpu.make_async_copy(tiles_hbm, tiles, tile_sem)
    load_tiles.start()

    barrier = pltpu.get_barrier_semaphore()
    peers = [sibling] + [device(dx=s) for s in (1, 2, 3)] + [device(dy=s) for s in (1, 2, 3)]
    peers += [along_z(s)[0] for s in range(1, 16)]
    for peer in peers:
        pl.semaphore_signal(barrier, inc=1, device_id=peer, device_id_type=MESH)

    grad = grad_ref[...] * mask_ref[...].astype(F32).astype(BF16)
    own = core * 8 + z
    for c in range(NCHUNK):
        gathered[c][own] = lax.dot_general(
            weight_ref[pl.ds(c * T, T), :], grad, (((1,), (1,)), ((), ())),
            preferred_element_type=F32,
        ).astype(BF16)
    pl.semaphore_wait(barrier, len(peers))

    spread, arrive, share = [], [], []
    for c in range(NCHUNK):
        sends, comes = [], []
        for step in range(1, 8):
            target, _ = along_group(step)
            sent = k.copy(gathered[c].at[own], gathered[c].at[own], target)
            sends.append(sent)
            _, source = along_group(8 - step)
            slot = gathered[c].at[core * 8 + source]
            comes.append(
                pltpu.make_async_remote_copy(
                    src_ref=slot, dst_ref=slot,
                    send_sem=send_sems.at[k.used - 1], recv_sem=recv_sems.at[k.used - 1],
                    device_id=target, device_id_type=MESH,
                )
            )
        spread.append(sends)
        arrive.append(comes)
        mine = gathered[c].at[pl.ds(core * 8, 8)]
        share.append(k.copy(mine, mine, sibling))

    def gather_start(c):
        for sent in spread[c]:
            sent.start()

    def gather_pass(c):
        for came in arrive[c]:
            came.wait_recv()
        share[c].start()

    def gather_done(c):
        share[c].wait_recv()

    gather_start(0)
    gather_start(1)

    for h in range(2):
        for q in range(4):
            wl[h, q] = lax.dot_general(
                agg_ref[:, h * 256:(h + 1) * 256], grad[:, q * T:(q + 1) * T],
                (((0,), (0,)), ((), ())), preferred_element_type=F32,
            ).astype(BF16)
    w_share = k.copy(wl.at[1 - core], ws, sibling)
    w_share.start()
    w_x = Ring(k, wa, 128, wxl, wxr, wxfl, wxfr, wb, right_x, left_x)
    w_y = Ring(k, wb, 32, wyl, wyr, wyfl, wyfr, wc, right_y, left_y)
    w_z = []
    w_z_comes = []
    for step in range(1, 16):
        target, _ = along_z(step)
        _, source = along_z(16 - step)
        w_z.append(k.copy(wz.at[zz], wz.at[zz], target))
        w_z_comes.append(
            pltpu.make_async_remote_copy(
                src_ref=wz.at[source], dst_ref=wz.at[source],
                send_sem=send_sems.at[k.used - 1], recv_sem=recv_sems.at[k.used - 1],
                device_id=target, device_id_type=MESH,
            )
        )
    w_back_y, w_back_y_comes, w_back_x, w_back_x_comes = [], [], [], []
    for step in range(1, 4):
        block = wg.at[core, x, y]
        w_back_y.append(k.copy(block, block, device(dy=step)))
        came = wg.at[core, x, wrap4(y + 4 - step)]
        w_back_y_comes.append(
            pltpu.make_async_remote_copy(
                src_ref=came, dst_ref=came,
                send_sem=send_sems.at[k.used - 1], recv_sem=recv_sems.at[k.used - 1],
                device_id=device(dy=step), device_id_type=MESH,
            )
        )
    for step in range(1, 4):
        block = wg.at[core, x]
        w_back_x.append(k.copy(block, block, device(dx=step)))
        came = wg.at[core, wrap4(x + 4 - step)]
        w_back_x_comes.append(
            pltpu.make_async_remote_copy(
                src_ref=came, dst_ref=came,
                send_sem=send_sems.at[k.used - 1], recv_sem=recv_sems.at[k.used - 1],
                device_id=device(dx=step), device_id_type=MESH,
            )
        )
    w_back_core = k.copy(wg.at[core], wg.at[core], sibling)
    w_back_core_came = pltpu.make_async_remote_copy(
        src_ref=wg.at[1 - core], dst_ref=wg.at[1 - core],
        send_sem=send_sems.at[k.used - 1], recv_sem=recv_sems.at[k.used - 1],
        device_id=sibling, device_id_type=MESH,
    )

    def weight_1():
        w_share.wait_recv()
        for a in range(4):
            xt = wrap4(x + a)
            for b in range(4):
                rows = pl.ds(pl.multiple_of(wrap4(y + b) * 64, 64), 64)
                wa[pl.ds(a * 256 + b * 64, 64)] = (
                    wl[core, xt, rows].astype(F32) + ws[xt, rows].astype(F32)
                ).astype(BF16)
        w_x.first()

    def weight_3():
        w_x.last()
        w_y.first()

    def weight_5():
        w_y.last()
        wz[zz] = wc[...]
        for sent in w_z:
            sent.start()

    def weight_6():
        for came in w_z_comes:
            came.wait_recv()
        total = wz[0].astype(F32)
        for place in range(1, 16):
            total = total + wz[place].astype(F32)
        wg[core, x, y] = total.astype(BF16)
        for sent in w_back_y:
            sent.start()

    def weight_7():
        for came in w_back_y_comes:
            came.wait_recv()
        for sent in w_back_x:
            sent.start()

    def weight_8():
        for came in w_back_x_comes:
            came.wait_recv()
        w_back_core.start()

    def weight_9():
        w_back_core_came.wait_recv()
        wgrad_ref[...] = wg[...]

    def compute(c, first, stop):
        def block(step, acc):
            for inner in range(UNROLL):
                p = first + step * UNROLL + inner
                product = jnp.dot(
                    gathered[c][order_ref[1, p]], tiles[order_ref[0, p]],
                    preferred_element_type=F32,
                )
                acc = acc * gate_ref[0, p] + product
                seg[p] = acc.astype(BF16)
            return acc

        if first == 0:
            start = jnp.zeros((T, T), F32)
        else:
            start = acc_ref[...]
        end = lax.fori_loop(0, (stop - first) // UNROLL, block, start)
        if stop < SLOTS:
            acc_ref[...] = end

    def place(c):
        def one(m, carry):
            major, minor = lax.div(m, 4), lax.rem(m, 4)
            rows = pl.ds(pl.multiple_of(m * T, T), T)
            for dt in range(2):
                a, b = (major, minor) if dt == 0 else (minor, major)
                target = (wrap4(x + a) * 4 + wrap4(y + b)) * 2 + dt
                parts[c, dt, rows] = (
                    seg[order_ref[2, target]].astype(F32) * gate_ref[1, target]
                ).astype(BF16)
            return carry

        lax.fori_loop(0, 16, one, 0)

    ring_a, ring_b, cross = [], [], []
    for c in range(NCHUNK):
        for dt in range(2):
            far = (right_x, left_x) if dt == 0 else (right_y, left_y)
            near = (right_y, left_y) if dt == 0 else (right_x, left_x)
            ring_a.append(Ring(
                k, parts.at[c, dt], 256, xl.at[c, dt], xr.at[c, dt], xfl.at[c, dt], xfr.at[c, dt],
                mids.at[c, dt], *far,
            ))
            ring_b.append(Ring(
                k, mids.at[c, dt], 64, yl.at[c, dt], yr.at[c, dt], yfl.at[c, dt], yfr.at[c, dt],
                tops.at[c, dt], *near,
            ))
        cross.append(k.copy(tops.at[c, 1 - depth], ztop.at[c], partner))

    def reduce_1(c):
        for dt in range(2):
            ring_a[2 * c + dt].first()

    def reduce_2(c):
        for dt in range(2):
            ring_a[2 * c + dt].second()

    def reduce_3(c):
        for dt in range(2):
            ring_a[2 * c + dt].last()
            ring_b[2 * c + dt].first()

    def reduce_4(c):
        for dt in range(2):
            ring_b[2 * c + dt].second()

    def reduce_5(c):
        for dt in range(2):
            ring_b[2 * c + dt].last()
        cross[c].start()

    def reduce_6(c):
        cross[c].wait_recv()
        node_ref[pl.ds(c * T, T)] = (
            tops[c, depth].astype(F32) + ztop[c].astype(F32)
        ).astype(BF16)

    gather_pass(0)
    gather_start(2)
    weight_1()
    load_tiles.wait()
    gather_done(0)
    compute(0, 0, HALF)
    w_x.second()
    compute(0, HALF, SLOTS)
    place(0)
    reduce_1(0)

    gather_pass(1)
    gather_start(3)
    weight_3()
    gather_done(1)
    compute(1, 0, HALF)
    reduce_2(0)
    w_y.second()
    compute(1, HALF, SLOTS)
    place(1)
    reduce_1(1)

    reduce_3(0)
    gather_pass(2)
    weight_5()
    gather_done(2)
    compute(2, 0, HALF)
    reduce_2(1)
    reduce_4(0)
    compute(2, HALF, SLOTS)
    place(2)
    reduce_1(2)

    reduce_3(1)
    reduce_5(0)
    gather_pass(3)
    weight_6()
    gather_done(3)
    compute(3, 0, HALF)
    reduce_2(2)
    reduce_4(1)
    compute(3, HALF, SLOTS)
    place(3)
    reduce_1(3)

    weight_7()
    reduce_3(2)
    reduce_5(1)
    reduce_6(0)
    reduce_2(3)
    reduce_4(2)
    weight_8()
    reduce_3(3)
    reduce_5(2)
    reduce_6(1)
    reduce_4(3)
    reduce_6(2)
    reduce_5(3)
    weight_9()
    reduce_6(3)
    for made in k.all:
        made.wait_send()


def on_device(
    grad_out, relu_mask, aggregated, weight, adjacency_tiles, tile_rows, tile_cols, tile_count
):
    slots = jnp.arange(SLOTS)
    key = jnp.where(slots < tile_count[0], tile_cols, GROUP)
    before = (key[None, :] < key[:, None]) | (
        (key[None, :] == key[:, None]) & (slots[None, :] < slots[:, None])
    )
    rank = jnp.sum(before.astype(jnp.int32), axis=1)
    picked = (rank[None, :] == slots[:, None]).astype(jnp.int32)
    order = jnp.sum(picked * slots[None, :], axis=1)
    place = (tile_rows % 2) * 8 + tile_rows // 2
    rows = jnp.sum(picked * place[None, :], axis=1)
    starts = jnp.sum(picked * jnp.sum(
        ((key[None, :] == key[:, None]) & (slots[None, :] < slots[:, None])).astype(jnp.int32), axis=1
    )[None, :], axis=1)
    keep = (starts > 0).astype(F32)
    groups = jnp.arange(SLOTS)
    upto = jnp.sum((key[None, :] <= groups[:, None]).astype(jnp.int32), axis=1)
    last = jnp.maximum(upto - 1, 0)
    has = jnp.max((key[None, :] == groups[:, None]).astype(F32), axis=1)
    order_all = jnp.stack([order, rows, last])
    gates = jnp.stack([keep, has])

    smem = pl.BlockSpec(memory_space=pltpu.SMEM)
    vmem = pl.BlockSpec(memory_space=pltpu.VMEM)
    bf = lambda *shape: pltpu.VMEM(shape, BF16)
    node_t, wgrad = pl.pallas_call(
        kernel,
        out_shape=(
            jax.ShapeDtypeStruct((NCHUNK * T, T), BF16),
            jax.ShapeDtypeStruct((2, 4, 4, 64, T), BF16),
        ),
        in_specs=[smem, smem, vmem, vmem, vmem, vmem, pl.BlockSpec(memory_space=pl.ANY)],
        out_specs=(vmem, vmem),
        scratch_shapes=[
            bf(SLOTS, T, T), bf(SLOTS, T, T), pltpu.VMEM((T, T), F32),
            bf(16, T, T), bf(16, T, T), bf(16, T, T), bf(16, T, T),
            bf(4, 2, 16 * T, T),
            bf(4, 2, 512, T), bf(4, 2, 512, T), bf(4, 2, 256, T), bf(4, 2, 256, T),
            bf(4, 2, 512, T),
            bf(4, 2, 128, T), bf(4, 2, 128, T), bf(4, 2, 64, T), bf(4, 2, 64, T),
            bf(4, 2, 128, T), bf(4, 128, T),
            bf(2, 4, 256, T), bf(4, 256, T), bf(1024, T),
            bf(256, T), bf(256, T), bf(128, T), bf(128, T),
            bf(256, T),
            bf(64, T), bf(64, T), bf(32, T), bf(32, T),
            bf(64, T), bf(16, 64, T), bf(2, 4, 4, 64, T),
            pltpu.SemaphoreType.DMA((SEMS,)),
            pltpu.SemaphoreType.DMA((SEMS,)),
            pltpu.SemaphoreType.DMA,
        ],
        compiler_params=pltpu.CompilerParams(
            collective_id=0, has_side_effects=True, vmem_limit_bytes=48 * 1024 * 1024
        ),
        cost_estimate=pl.CostEstimate(flops=1_600_000_000, bytes_accessed=5_000_000, transcendentals=0),
    )(order_all, gates, grad_out, relu_mask, aggregated, weight, adjacency_tiles)
    node_grad = node_t.T
    weight_grad = wgrad.transpose(0, 2, 3, 1, 4).reshape(512, 512).astype(F32)
    return (node_grad, weight_grad)


def solution(mesh):
    return jax.shard_map(
        on_device,
        mesh=mesh,
        in_specs=(
            P(("row", "col", "depth"), None),
            P(("row", "col", "depth"), None),
            P(("row", "col", "depth"), None),
            P(),
            P(("row", "col", "depth"), None, None),
            P(("row", "col", "depth")),
            P(("row", "col", "depth")),
            P(("row", "col", "depth")),
        ),
        out_specs=(P(("row", "col", "depth"), None), P()),
        check_vma=False,
    )
```

time: 692 us -> 125 us (0.18)
  the two profiles are of different devices: /device:TPU:1 before, /device:TPU:448 now
where the time goes in v1:
time: 125 us
  Pallas kernels  114 us (91%)
  local copies, waits for them, and re-layouts  8.06 us (6%)
  other arithmetic  1.9 us (2%)
  between operations  1.35 us (1%)
    pallas_call x1, Pallas kernels, on_device(): pl.pallas_call(kernel, out_shape=(jax.ShapeDtypeStruct((NCHUNK * T, T), B...  114 us
    unnamed x12, local copies, waits for them, and re-layouts  7.38 us

profile of v1, /device:TPU:448, one launch (start us, length us, event | category | flops | bytes accessed | tf_op | source)
XLA Modules:
  0.0 125.1 jit_solution(5561376553191084306)
XLA Ops:
  1.3 0.7 compare_select_fusion
  1.9 0.7 fusion.2
  2.6 0.1 convert_reduce_fusion
  2.7 0.2 convert_reduce_fusion.1
  2.9 0.2 select_reduce_fusion
  3.1 0.0 copy-start
  3.1 1.8 %copy-done = bf16[84,128,128]{2,1,0:T(8,128)(2,1)S(1)} copy-done((bf16[84,128,128]{2,1,0:T(8,128)(2,1)S(1)}, bf16[84,128,128]{2,1,0:T(8,128)(2,1)}, u32[]{:S(2)}) %copy-start) | copy-done | bytes 2752536
  4.9 0.0 copy-start.1
  4.9 1.0 copy-done.1
  5.9 0.0 copy-start.2
  5.9 0.9 copy-done.2
  6.9 0.0 copy-start.3
  6.9 0.9 copy-done.3
  7.8 0.0 copy-start.4
  7.8 0.9 copy-done.4
  8.7 113.8 %shard_map.95 = (bf16[512,128]{1,0:T(8,128)(2,1)S(1)}, bf16[2,4,4,64,128]{4,3,2,1,0:T(8,128)(2,1)S(1)}) custom-call(s32[3,84]{1,0:T(4,128)S(1)} %pad_add_fusion.order_ref, f32[2,84]{1,0:T(2,128)S(1)} %pad_maximum_fusion.gate_ref, bf16[128,512]{1,0:T(8,128)(2,1)S(1)} %copy-done.3, s32[128,512]{1,0:T(8,128)S(1)} %copy-done.2, bf16[128,512]{1,0:T(8,128)(2,1)S(1)} %copy-done.4, ...), custom_call_target="tpu_custom_call" | custom-call | flops 1600000000 | bytes 5000000 | tf_op jit(solution)/shard_map/pallas_call | solution.py:440
  122.5 0.8 copy.14
  123.3 0.1 convert_bitcast_fusion
  123.4 0.7 copy.13
  124.1 1.0 copy.17
  (4 shorter events, 0.0 us)
Async XLA Ops:
  3.1 1.8 %copy-start = (bf16[84,128,128]{2,1,0:T(8,128)(2,1)S(1)}, bf16[84,128,128]{2,1,0:T(8,128)(2,1)}, u32[]{:S(2)}) copy-start(bf16[84,128,128]{2,1,0:T(8,128)(2,1)} %tiles_hbm.1) | copy-start | bytes 8257540
  4.9 1.0 copy-start.1
  5.9 0.9 copy-start.2
  6.9 0.9 copy-start.3
  7.8 0.9 copy-start.4

commit v2 on v1

v2 whole, which is shorter than its diff:
```python
import jax
import jax.numpy as jnp
from jax import lax
from jax.experimental import pallas as pl
from jax.experimental.pallas import tpu as pltpu
from jax.sharding import PartitionSpec as P

MESH = pl.DeviceIdType.MESH
F32 = jnp.float32
BF16 = jnp.bfloat16
T = 128
NCHUNK = 4
SLOTS = 84
GROUP = 32
UNROLL = 6
HALF = SLOTS // 2
SEMS = 200


def wrap4(value):
    return lax.rem(value, 4)


class Ring:
    def __init__(self, k, src, unit, rl, rr, fl, fr, out, right, left):
        self.src, self.unit, self.out = src, unit, out
        self.rl, self.rr, self.fl, self.fr = rl, rr, fl, fr
        u = unit
        self.to_right = k.copy(src.at[pl.ds(3 * u, 2 * u)], rl, right)
        self.to_left = k.copy(src.at[pl.ds(5 * u, 2 * u)], rr, left)
        self.sum_right = k.copy(src.at[pl.ds(2 * u, u)], fl, right)
        self.sum_left = k.copy(src.at[pl.ds(7 * u, u)], fr, left)

    def first(self):
        self.to_right.start()
        self.to_left.start()

    def second(self):
        u, src = self.unit, self.src
        self.to_right.wait_recv()
        src[pl.ds(2 * u, u)] = (
            src[pl.ds(2 * u, u)].astype(F32) + self.rl[pl.ds(u, u)].astype(F32)
        ).astype(BF16)
        self.sum_right.start()
        self.to_left.wait_recv()
        src[pl.ds(7 * u, u)] = (
            src[pl.ds(7 * u, u)].astype(F32) + self.rr[pl.ds(0, u)].astype(F32)
        ).astype(BF16)
        self.sum_left.start()

    def last(self):
        u, src = self.unit, self.src
        self.sum_right.wait_recv()
        self.out[pl.ds(0, u)] = (
            src[pl.ds(0, u)].astype(F32)
            + self.fl[...].astype(F32)
            + self.rr[pl.ds(u, u)].astype(F32)
        ).astype(BF16)
        self.sum_left.wait_recv()
        self.out[pl.ds(u, u)] = (
            src[pl.ds(u, u)].astype(F32)
            + self.rl[pl.ds(0, u)].astype(F32)
            + self.fr[...].astype(F32)
        ).astype(BF16)


class Fan:
    def __init__(self, k, src, unit, landed, devices):
        self.src, self.unit, self.landed = src, unit, landed
        self.sends = [
            k.copy(src.at[pl.ds(s * unit, unit)], landed.at[pl.ds((s - 1) * unit, unit)], devices[s - 1])
            for s in (1, 2, 3)
        ]

    def first(self):
        for s in (1, 0, 2):
            self.sends[s].start()

    def arrived(self):
        for sent in self.sends:
            sent.wait_recv()


class Copies:
    def __init__(self, send_sems, recv_sems):
        self.send_sems, self.recv_sems, self.used = send_sems, recv_sems, 0
        self.all = []

    def copy(self, src, dst, device):
        index = self.used
        self.used += 1
        made = pltpu.make_async_remote_copy(
            src_ref=src,
            dst_ref=dst,
            send_sem=self.send_sems.at[index],
            recv_sem=self.recv_sems.at[index],
            device_id=device,
            device_id_type=MESH,
        )
        self.all.append(made)
        return made

    def swap(self, src, dst, device):
        sent = self.copy(src, src, device)
        came = pltpu.make_async_remote_copy(
            src_ref=dst,
            dst_ref=dst,
            send_sem=self.send_sems.at[self.used - 1],
            recv_sem=self.recv_sems.at[self.used - 1],
            device_id=device,
            device_id_type=MESH,
        )
        return sent, came


def kernel(
    count_ref, rows_ref, cols_ref, grad_hbm, mask_hbm, agg_hbm, weight_hbm, tiles_hbm,
    node_ref, wgrad_ref,
    grad_v, mask_v, agg_v, weight_v,
    tiles, seg, acc_ref,
    g0, g1, g2, g3,
    parts, xl, xr, xfl, xfr, mids, landed, tops, ztop,
    wl, ws, wa, wxl, wxr, wxfl, wxfr, wb, wyl, wyr, wyfl, wyfr, wc, wq, wn, wg,
    lists, places, gates, place_s, gate_s,
    send_sems, recv_sems, line_send, line_recv, share_send, share_recv, local_sems,
):
    row, col, depth = lax.axis_index("row"), lax.axis_index("col"), lax.axis_index("depth")
    x, y = lax.div(row, 4), lax.rem(row, 4)
    z, core = lax.div(col, 2), lax.rem(col, 2)
    zz = depth * 8 + z
    quad = lax.rem(z, 4)
    quads = lax.div(zz, 4)
    gathered = (g0, g1, g2, g3)

    def device(dx=0, dy=0):
        return (wrap4(x + dx) * 4 + wrap4(y + dy), col, depth)

    def along_z(step):
        place = lax.rem(zz + step, 16)
        return (row, lax.rem(place, 8) * 2 + core, lax.div(place, 8))

    def in_quad(step):
        return (row, (z - quad + wrap4(quad + step)) * 2 + core, depth)

    sibling = (row, z * 2 + 1 - core, depth)
    right_x, left_x = device(dx=1), device(dx=3)
    right_y, left_y = device(dy=1), device(dy=3)
    all_x = [device(dx=s) for s in (1, 2, 3)]
    all_y = [device(dy=s) for s in (1, 2, 3)]
    partner = (row, col, 1 - depth)
    k = Copies(send_sems, recv_sems)

    loads = [
        pltpu.make_async_copy(src, dst, local_sems.at[i])
        for i, (src, dst) in enumerate((
            (grad_hbm, grad_v), (mask_hbm, mask_v), (weight_hbm, weight_v), (agg_hbm, agg_v), (tiles_hbm, tiles),
        ))
    ]
    for load in loads:
        load.start()

    barrier = pltpu.get_barrier_semaphore()
    peers = [sibling] + all_x + all_y + [along_z(s) for s in (1, 15, 2, 14, 4, 8, 12)]
    peers += [in_quad(s) for s in (1, 2, 3)]
    for peer in peers:
        pl.semaphore_signal(barrier, inc=1, device_id=peer, device_id_type=MESH)

    for load in loads[:3]:
        load.wait()
    grad_v[...] = grad_v[...] * mask_v[...].astype(F32).astype(BF16)
    own = core * 8 + z
    for c in range(NCHUNK):
        gathered[c][own] = lax.dot_general(
            weight_v[pl.ds(c * T, T), :], grad_v[...], (((1,), (1,)), ((), ())),
            preferred_element_type=F32,
        ).astype(BF16)
    pl.semaphore_wait(barrier, len(peers))

    def there(place):
        return (place >= 0) & (place <= 7)

    def line(c, source, sign, hop, device=None):
        block = gathered[c].at[core * 8 + source]
        return pltpu.make_async_remote_copy(
            src_ref=block, dst_ref=block,
            send_sem=line_send.at[c, source, hop + (1 if sign > 0 else -1)],
            recv_sem=line_recv.at[c, source],
            device_id=device or (row, (z + sign * hop) * 2 + core, depth), device_id_type=MESH,
        )

    def share(c, source, side):
        block = gathered[c].at[side * 8 + source]
        return pltpu.make_async_remote_copy(
            src_ref=block, dst_ref=block,
            send_sem=share_send.at[c, source], recv_sem=share_recv.at[c, source],
            device_id=sibling, device_id_type=MESH,
        )

    def each_send(c, source, sign, act):
        for hop in (2, 1):
            @pl.when(there(z + sign * hop))
            def _():
                act(line(c, source, sign, hop))

    def begin(c):
        for sign in (1, -1):
            each_send(c, z, sign, lambda made: made.start())
        share(c, z, core).start()

    def forward(c, m):
        for sign in (1, -1):
            source = z - sign * 2 * m

            @pl.when(there(source))
            def _():
                line(c, source, sign, 1, sibling).wait_recv()
                each_send(c, source, sign, lambda made: made.start())
                share(c, source, core).start()

    def deliver(c):
        for m in range(4):
            for sign in (1, -1):
                source = z - sign * (2 * m + 1)

                @pl.when(there(source))
                def _():
                    line(c, source, sign, 1, sibling).wait_recv()
                    share(c, source, core).start()

    def shared(c):
        for source in range(8):
            share(c, source, 1 - core).wait_recv()

    def line_end():
        for c in range(NCHUNK):
            for m in range(4):
                for sign in (1, -1):
                    source = z - sign * 2 * m

                    @pl.when(there(source))
                    def _():
                        each_send(c, source, sign, lambda made: made.wait_send())
            for source in range(8):
                share(c, source, core).wait_send()

    w_share = k.copy(wl.at[1 - core], ws, sibling)
    w_x = Ring(k, wa, 128, wxl, wxr, wxfl, wxfr, wb, right_x, left_x)
    w_y = Ring(k, wb, 32, wyl, wyr, wyfl, wyfr, wc, right_y, left_y)
    w_q = [
        k.copy(wc.at[pl.ds(pl.multiple_of(wrap4(quad + s) * 16, 16), 16)], wq.at[s - 1], in_quad(s))
        for s in (1, 2, 3)
    ]
    w_n = [
        k.swap(wn.at[quads], wn.at[wrap4(quads + 4 - s)], along_z(4 * s)) for s in (1, 2, 3)
    ]

    def strip(place):
        return wg.at[core, x, y, pl.ds(pl.multiple_of(place * 16, 16), 16)]

    w_back_q = [k.swap(strip(quad), strip(wrap4(quad + 4 - s)), in_quad(s)) for s in (1, 2, 3)]
    w_back_y = [
        k.swap(wg.at[core, x, y], wg.at[core, x, wrap4(y + 4 - s)], device(dy=s)) for s in (1, 2, 3)
    ]
    w_back_x = [
        k.swap(wg.at[core, x], wg.at[core, wrap4(x + 4 - s)], device(dx=s)) for s in (1, 2, 3)
    ]
    w_back_core = k.swap(wg.at[core], wg.at[1 - core], sibling)

    def weight_0():
        loads[3].wait()
        for h in range(2):
            for q in range(4):
                wl[h, q] = lax.dot_general(
                    agg_v[:, h * 256:(h + 1) * 256], grad_v[:, q * T:(q + 1) * T],
                    (((0,), (0,)), ((), ())), preferred_element_type=F32,
                ).astype(BF16)
        w_share.start()

    def weight_1():
        w_share.wait_recv()
        for a in range(4):
            xt = wrap4(x + a)
            for b in range(4):
                rows = pl.ds(pl.multiple_of(wrap4(y + b) * 64, 64), 64)
                wa[pl.ds(a * 256 + b * 64, 64)] = (
                    wl[core, xt, rows].astype(F32) + ws[xt, rows].astype(F32)
                ).astype(BF16)
        w_x.first()

    def weight_2():
        w_x.second()

    def weight_3():
        w_x.last()
        w_y.first()

    def weight_4():
        w_y.second()

    def weight_5():
        w_y.last()
        for sent in w_q:
            sent.start()

    def weight_6():
        total = wc[pl.ds(pl.multiple_of(quad * 16, 16), 16)].astype(F32)
        for s in range(3):
            w_q[s].wait_recv()
            total = total + wq[s].astype(F32)
        wn[quads] = total.astype(BF16)
        for sent, _ in w_n:
            sent.start()

    def weight_7():
        for _, came in w_n:
            came.wait_recv()
        total = wn[0].astype(F32)
        for place in range(1, 4):
            total = total + wn[place].astype(F32)
        wg[core, x, y, pl.ds(pl.multiple_of(quad * 16, 16), 16)] = total.astype(BF16)
        for sent, _ in w_back_q:
            sent.start()

    def weight_8():
        for _, came in w_back_q:
            came.wait_recv()
        for sent, _ in w_back_y:
            sent.start()

    def weight_9():
        for _, came in w_back_y:
            came.wait_recv()
        for sent, _ in w_back_x:
            sent.start()

    def weight_10():
        for _, came in w_back_x:
            came.wait_recv()
        w_back_core[0].start()

    def weight_11():
        w_back_core[1].wait_recv()
        for h in range(2):
            for a in range(4):
                for b in range(4):
                    wgrad_ref[pl.ds(h * 256 + b * 64, 64), a * T:(a + 1) * T] = wg[h, a, b]

    def sort():
        lane = lax.broadcasted_iota(jnp.int32, (1, T), 1)
        lists[...] = jnp.zeros((8, T), jnp.int32)
        lists[0:1, 0:SLOTS] = cols_ref[...]
        lists[1:2, 0:SLOTS] = rows_ref[...]
        key = jnp.where(lane < count_ref[0], lists[0:1, :], GROUP)
        key = jnp.where(lane < SLOTS, key, GROUP)
        tile_row = lists[1:2, :]
        slab_place = (tile_row & 1) * 8 + (tile_row >> 1)
        above = lax.broadcasted_iota(jnp.int32, (T, T), 0)
        across = lax.broadcasted_iota(jnp.int32, (T, T), 1)

        def wide(value):
            return jnp.broadcast_to(value, (T, T))

        def count(mask, value=1):
            return jnp.sum(jnp.where(mask, value, 0), axis=0, keepdims=True)

        key_a = wide(key)
        key_t = key_a.T
        same = (key_t == key_a) & (above < across)
        rank = count((key_t < key_a) | same)
        follows = jnp.minimum(count(same), 1)
        chosen = wide(rank).T == across
        places[0:1, :] = jnp.minimum(count(chosen, above), SLOTS - 1)
        places[1:2, :] = jnp.minimum(count(chosen, wide(slab_place).T), 15)
        places[2:3, :] = jnp.clip(count(key_t <= across) - 1, 0, SLOTS - 1)
        gates[0:1, :] = count(chosen, wide(follows).T).astype(F32)
        gates[1:2, :] = jnp.minimum(count(key_t == across), 1).astype(F32)
        for made in (
            pltpu.make_async_copy(places, place_s, local_sems.at[5]),
            pltpu.make_async_copy(gates, gate_s, local_sems.at[6]),
        ):
            made.start()
            made.wait()

    def compute(c, first, stop):
        def block(step, acc):
            for inner in range(UNROLL):
                p = first + step * UNROLL + inner
                product = jnp.dot(
                    gathered[c][place_s[1, p]], tiles[place_s[0, p]],
                    preferred_element_type=F32,
                )
                acc = acc * gate_s[0, p] + product
                seg[p] = acc.astype(BF16)
            return acc

        if first == 0:
            start = jnp.zeros((T, T), F32)
        else:
            start = acc_ref[...]
        end = lax.fori_loop(0, (stop - first) // UNROLL, block, start)
        if stop < SLOTS:
            acc_ref[...] = end

    def place(c):
        def one(m, carry):
            major, minor = lax.div(m, 4), lax.rem(m, 4)
            rows = pl.ds(pl.multiple_of(m * T, T), T)
            for dt in range(2):
                a, b = (major, minor) if dt == 0 else (minor, major)
                target = (wrap4(x + a) * 4 + wrap4(y + b)) * 2 + dt
                parts[c, dt, rows] = (
                    seg[place_s[2, target]].astype(F32) * gate_s[1, target]
                ).astype(BF16)
            return carry

        lax.fori_loop(0, 16, one, 0)

    ring, fan, cross = [], [], []
    for c in range(NCHUNK):
        for dt in range(2):
            far = (right_x, left_x) if dt == 0 else (right_y, left_y)
            ring.append(Ring(
                k, parts.at[c, dt], 256, xl.at[c, dt], xr.at[c, dt], xfl.at[c, dt], xfr.at[c, dt],
                mids.at[c, dt], *far,
            ))
            fan.append(Fan(k, mids.at[c, dt], T, landed.at[c, dt], all_y if dt == 0 else all_x))
        cross.append(k.copy(tops.at[c, 1 - depth], ztop.at[c], partner))

    def reduce_1(c):
        for dt in range(2):
            ring[2 * c + dt].first()

    def reduce_2(c):
        for dt in range(2):
            ring[2 * c + dt].second()

    def reduce_3(c):
        for dt in range(2):
            ring[2 * c + dt].last()
            fan[2 * c + dt].first()

    def reduce_4(c):
        for dt in range(2):
            fan[2 * c + dt].arrived()
        for turn, dt in enumerate((1 - depth, depth)):
            total = mids[c, dt, 0:T].astype(F32)
            for s in range(3):
                total = total + landed[c, dt, s * T:(s + 1) * T].astype(F32)
            tops[c, dt] = total.astype(BF16)
            if turn == 0:
                cross[c].start()

    def reduce_5(c):
        cross[c].wait_recv()
        node_ref[pl.ds(c * T, T)] = (
            tops[c, depth].astype(F32) + ztop[c].astype(F32)
        ).astype(BF16)

    begin(0)
    begin(1)
    sort()
    weight_0()
    forward(0, 1)
    begin(2)
    forward(1, 1)
    weight_1()
    forward(0, 2)
    forward(1, 2)
    begin(3)
    forward(2, 1)
    weight_2()
    forward(0, 3)
    deliver(0)
    forward(1, 3)
    forward(2, 2)
    forward(3, 1)
    loads[4].wait()
    shared(0)

    compute(0, 0, HALF)
    weight_3()
    forward(2, 3)
    forward(3, 2)
    compute(0, HALF, SLOTS)
    place(0)
    reduce_1(0)
    deliver(1)
    forward(3, 3)
    shared(1)

    compute(1, 0, HALF)
    reduce_2(0)
    weight_4()
    compute(1, HALF, SLOTS)
    place(1)
    reduce_1(1)
    deliver(2)
    reduce_3(0)
    shared(2)

    compute(2, 0, HALF)
    reduce_2(1)
    weight_5()
    reduce_4(0)
    compute(2, HALF, SLOTS)
    place(2)
    reduce_1(2)
    deliver(3)
    reduce_3(1)
    weight_6()
    shared(3)

    compute(3, 0, HALF)
    reduce_2(2)
    weight_7()
    reduce_4(1)
    compute(3, HALF, SLOTS)
    place(3)
    reduce_1(3)

    weight_8()
    reduce_3(2)
    reduce_5(0)
    weight_9()
    reduce_2(3)
    reduce_4(2)
    weight_10()
    reduce_3(3)
    reduce_5(1)
    weight_11()
    reduce_4(3)
    reduce_5(2)
    reduce_5(3)
    for made in k.all:
        made.wait_send()
    line_end()


def on_device(
    grad_out, relu_mask, aggregated, weight, adjacency_tiles, tile_rows, tile_cols, tile_count
):
    smem = pl.BlockSpec(memory_space=pltpu.SMEM)
    vmem = pl.BlockSpec(memory_space=pltpu.VMEM)
    hbm = pl.BlockSpec(memory_space=pltpu.HBM)
    bf = lambda *shape: pltpu.VMEM(shape, BF16)
    node_t, wgrad = pl.pallas_call(
        kernel,
        out_shape=(
            jax.ShapeDtypeStruct((NCHUNK * T, T), BF16),
            jax.ShapeDtypeStruct((512, 512), BF16),
        ),
        in_specs=[smem, vmem, vmem, hbm, hbm, hbm, hbm, hbm],
        out_specs=(vmem, vmem),
        scratch_shapes=[
            bf(T, 512), pltpu.VMEM((T, 512), jnp.int32), bf(T, 512), bf(512, 512),
            bf(SLOTS, T, T), bf(SLOTS, T, T), pltpu.VMEM((T, T), F32),
            bf(16, T, T), bf(16, T, T), bf(16, T, T), bf(16, T, T),
            bf(4, 2, 16 * T, T),
            bf(4, 2, 512, T), bf(4, 2, 512, T), bf(4, 2, 256, T), bf(4, 2, 256, T),
            bf(4, 2, 512, T),
            bf(4, 2, 3 * T, T),
            bf(4, 2, T, T), bf(4, T, T),
            bf(2, 4, 256, T), bf(4, 256, T), bf(1024, T),
            bf(256, T), bf(256, T), bf(128, T), bf(128, T),
            bf(256, T),
            bf(64, T), bf(64, T), bf(32, T), bf(32, T),
            bf(64, T), bf(3, 16, T), bf(4, 16, T), bf(2, 4, 4, 64, T),
            pltpu.VMEM((8, T), jnp.int32), pltpu.VMEM((8, T), jnp.int32), pltpu.VMEM((8, T), F32),
            pltpu.SMEM((8, T), jnp.int32), pltpu.SMEM((8, T), F32),
            pltpu.SemaphoreType.DMA((SEMS,)),
            pltpu.SemaphoreType.DMA((SEMS,)),
            pltpu.SemaphoreType.DMA((4, 8, 4)),
            pltpu.SemaphoreType.DMA((4, 8)),
            pltpu.SemaphoreType.DMA((4, 8)),
            pltpu.SemaphoreType.DMA((4, 8)),
            pltpu.SemaphoreType.DMA((7,)),
        ],
        compiler_params=pltpu.CompilerParams(
            collective_id=0, has_side_effects=True, vmem_limit_bytes=60 * 1024 * 1024
        ),
        cost_estimate=pl.CostEstimate(flops=1_600_000_000, bytes_accessed=5_000_000, transcendentals=0),
    )(
        tile_count, tile_rows.reshape(1, SLOTS), tile_cols.reshape(1, SLOTS),
        grad_out, relu_mask, aggregated, weight, adjacency_tiles,
    )
    return (node_t.T, wgrad.astype(F32))


def solution(mesh):
    return jax.shard_map(
        on_device,
        mesh=mesh,
        in_specs=(
            P(("row", "col", "depth"), None),
            P(("row", "col", "depth"), None),
            P(("row", "col", "depth"), None),
            P(),
            P(("row", "col", "depth"), None, None),
            P(("row", "col", "depth")),
            P(("row", "col", "depth")),
            P(("row", "col", "depth")),
        ),
        out_specs=(P(("row", "col", "depth"), None), P()),
        check_vma=False,
    )
```

time: 125 us -> 105 us (0.84)
  the two profiles are of different devices: /device:TPU:448 before, /device:TPU:1 now
where the time goes in v2:
time: 105 us; the launch traced here: 104 us
  Pallas kernels  98.4 us (94%)
  other arithmetic  2.14 us (2%)
  local copies, waits for them, and re-layouts  1.67 us (2%)
  between operations  1.29 us (1%)
    pallas_call x1, Pallas kernels, on_device(): pl.pallas_call(kernel, out_shape=(jax.ShapeDtypeStruct((NCHUNK * T, T), B...  98.4 us
    convert_element_type x1, other arithmetic, on_device(): return (node_t.T, wgrad.astype(F32))  2.14 us

profile of v2, /device:TPU:1, one launch (start us, length us, event | category | flops | bytes accessed | tf_op | source)
XLA Modules:
  0.0 103.5 jit_solution(3870514191626695770)
XLA Ops:
  1.3 98.4 %shard_map.95 = (bf16[512,128]{1,0:T(8,128)(2,1)}, bf16[512,512]{1,0:T(8,128)(2,1)}) custom-call(s32[1]{0:T(128)S(6)} %copy.11.count_ref, s32[1,84]{1,0:T(1,128)} %bitcast.4, s32[1,84]{1,0:T(1,128)} %bitcast.5, bf16[128,512]{1,0:T(8,128)(2,1)} %grad_hbm.1, s32[128,512]{1,0:T(8,128)} %mask_hbm.1, bf16[128,512]{1,0:T(8,128)(2,1)} %agg_hbm.1, ...), custom_call_target="tpu_custom_call" | custom-call | flops 1600000000 | bytes 5000000 | tf_op jit(solution)/shard_map/pallas_call | solution.py:546
  99.7 1.7 %copy.10 = bf16[128,512]{1,0:T(8,128)(2,1)} copy(bf16[128,512]{0,1:T(8,128)(2,1)} %bitcast.3) | data formatting | bytes 262144
  101.4 2.1 %convert_element_type.3 = f32[512,512]{1,0:T(8,128)} convert(bf16[512,512]{1,0:T(8,128)(2,1)} %get-tuple-element.5) | non-fusion elementwise | flops 262144 | bytes 1572864 | tf_op jit(solution)/shard_map/convert_element_type | solution.py:586

commit v3 on v2

--- a/solution.py
+++ b/solution.py
@@ -9,12 +9,14 @@
 F32 = jnp.float32
 BF16 = jnp.bfloat16
 T = 128
-NCHUNK = 4
+CHUNKS = (128, 128, 128, 128)
+NCHUNK = len(CHUNKS)
+STARTS = tuple(sum(CHUNKS[:c]) for c in range(NCHUNK))
 SLOTS = 84
 GROUP = 32
 UNROLL = 6
 HALF = SLOTS // 2
-SEMS = 200
+SEMS = 112
 
 
 def wrap4(value):
@@ -34,6 +36,10 @@
     def first(self):
         self.to_right.start()
         self.to_left.start()
+
+    def settle(self):
+        for sent in (self.to_right, self.to_left, self.sum_right, self.sum_left):
+            sent.wait_send()
 
     def second(self):
         u, src = self.unit, self.src
@@ -76,15 +82,25 @@
         for s in (1, 0, 2):
             self.sends[s].start()
 
+    def settle(self):
+        for sent in self.sends:
+            sent.wait_send()
+
     def arrived(self):
         for sent in self.sends:
             sent.wait_recv()
 
+    def total(self):
+        u = self.unit
+        value = self.src[pl.ds(0, u)].astype(F32)
+        for s in range(3):
+            value = value + self.landed[pl.ds(s * u, u)].astype(F32)
+        return value
+
 
 class Copies:
     def __init__(self, send_sems, recv_sems):
         self.send_sems, self.recv_sems, self.used = send_sems, recv_sems, 0
-        self.all = []
 
     def copy(self, src, dst, device):
         index = self.used
@@ -97,7 +113,6 @@
             device_id=device,
             device_id_type=MESH,
         )
-        self.all.append(made)
         return made
 
     def swap(self, src, dst, device):
@@ -118,9 +133,8 @@
     node_ref, wgrad_ref,
     grad_v, mask_v, agg_v, weight_v,
     tiles, seg, acc_ref,
-    g0, g1, g2, g3,
-    parts, xl, xr, xfl, xfr, mids, landed, tops, ztop,
-    wl, ws, wa, wxl, wxr, wxfl, wxfr, wb, wyl, wyr, wyfl, wyfr, wc, wq, wn, wg,
+    gathered, parts, xl, xr, xfl, xfr, mids, landed, tops, ztop,
+    wl, ws, wa, wxd, wb, wyd, wc, wq, wn, wg,
     lists, places, gates, place_s, gate_s,
     send_sems, recv_sems, line_send, line_recv, share_send, share_recv, local_sems,
 ):
@@ -130,7 +144,6 @@
     zz = depth * 8 + z
     quad = lax.rem(z, 4)
     quads = lax.div(zz, 4)
-    gathered = (g0, g1, g2, g3)
 
     def device(dx=0, dy=0):
         return (wrap4(x + dx) * 4 + wrap4(y + dy), col, depth)
@@ -171,7 +184,7 @@
     own = core * 8 + z
     for c in range(NCHUNK):
         gathered[c][own] = lax.dot_general(
-            weight_v[pl.ds(c * T, T), :], grad_v[...], (((1,), (1,)), ((), ())),
+            weight_v[pl.ds(STARTS[c], CHUNKS[c]), :], grad_v[...], (((1,), (1,)), ((), ())),
             preferred_element_type=F32,
         ).astype(BF16)
     pl.semaphore_wait(barrier, len(peers))
@@ -188,11 +201,11 @@
             device_id=device or (row, (z + sign * hop) * 2 + core, depth), device_id_type=MESH,
         )
 
-    def share(c, source, side):
-        block = gathered[c].at[side * 8 + source]
+    def share(c, side):
+        half = gathered[c].at[pl.ds(side * 8, 8)]
         return pltpu.make_async_remote_copy(
-            src_ref=block, dst_ref=block,
-            send_sem=share_send.at[c, source], recv_sem=share_recv.at[c, source],
+            src_ref=half, dst_ref=half,
+            send_sem=share_send.at[c], recv_sem=share_recv.at[c],
             device_id=sibling, device_id_type=MESH,
         )
 
@@ -205,7 +218,6 @@
     def begin(c):
         for sign in (1, -1):
             each_send(c, z, sign, lambda made: made.start())
-        share(c, z, core).start()
 
     def forward(c, m):
         for sign in (1, -1):
@@ -215,7 +227,6 @@
             def _():
                 line(c, source, sign, 1, sibling).wait_recv()
                 each_send(c, source, sign, lambda made: made.start())
-                share(c, source, core).start()
 
     def deliver(c):
         for m in range(4):
@@ -225,27 +236,24 @@
                 @pl.when(there(source))
                 def _():
                     line(c, source, sign, 1, sibling).wait_recv()
-                    share(c, source, core).start()
+        share(c, core).start()
 
     def shared(c):
-        for source in range(8):
-            share(c, source, 1 - core).wait_recv()
-
-    def line_end():
-        for c in range(NCHUNK):
-            for m in range(4):
-                for sign in (1, -1):
-                    source = z - sign * 2 * m
-
-                    @pl.when(there(source))
-                    def _():
-                        each_send(c, source, sign, lambda made: made.wait_send())
-            for source in range(8):
-                share(c, source, core).wait_send()
+        share(c, 1 - core).wait_recv()
+
+    def line_end(c):
+        for m in range(4):
+            for sign in (1, -1):
+                source = z - sign * 2 * m
+
+                @pl.when(there(source))
+                def _():
+                    each_send(c, source, sign, lambda made: made.wait_send())
+        share(c, core).wait_send()
 
     w_share = k.copy(wl.at[1 - core], ws, sibling)
-    w_x = Ring(k, wa, 128, wxl, wxr, wxfl, wxfr, wb, right_x, left_x)
-    w_y = Ring(k, wb, 32, wyl, wyr, wyfl, wyfr, wc, right_y, left_y)
+    w_x = Fan(k, wa, 256, wxd, all_x)
+    w_y = Fan(k, wb, 64, wyd, all_y)
     w_q = [
         k.copy(wc.at[pl.ds(pl.multiple_of(wrap4(quad + s) * 16, 16), 16)], wq.at[s - 1], in_quad(s))
         for s in (1, 2, 3)
@@ -286,23 +294,22 @@
                     wl[core, xt, rows].astype(F32) + ws[xt, rows].astype(F32)
                 ).astype(BF16)
         w_x.first()
+        w_share.wait_send()
 
     def weight_2():
-        w_x.second()
+        w_x.arrived()
+        wb[...] = w_x.total().astype(BF16)
+        w_y.first()
+        w_x.settle()
 
     def weight_3():
-        w_x.last()
-        w_y.first()
-
-    def weight_4():
-        w_y.second()
-
-    def weight_5():
-        w_y.last()
+        w_y.arrived()
+        wc[...] = w_y.total().astype(BF16)
         for sent in w_q:
             sent.start()
-
-    def weight_6():
+        w_y.settle()
+
+    def weight_4():
         total = wc[pl.ds(pl.multiple_of(quad * 16, 16), 16)].astype(F32)
         for s in range(3):
             w_q[s].wait_recv()
@@ -310,8 +317,10 @@
         wn[quads] = total.astype(BF16)
         for sent, _ in w_n:
             sent.start()
-
-    def weight_7():
+        for sent in w_q:
+            sent.wait_send()
+
+    def weight_5():
         for _, came in w_n:
             came.wait_recv()
         total = wn[0].astype(F32)
@@ -320,26 +329,35 @@
         wg[core, x, y, pl.ds(pl.multiple_of(quad * 16, 16), 16)] = total.astype(BF16)
         for sent, _ in w_back_q:
             sent.start()
-
-    def weight_8():
+        for sent, _ in w_n:
+            sent.wait_send()
+
+    def weight_6():
         for _, came in w_back_q:
             came.wait_recv()
         for sent, _ in w_back_y:
             sent.start()
-
-    def weight_9():
+        for sent, _ in w_back_q:
+            sent.wait_send()
+
+    def weight_7():
         for _, came in w_back_y:
             came.wait_recv()
         for sent, _ in w_back_x:
             sent.start()
-
-    def weight_10():
+        for sent, _ in w_back_y:
+            sent.wait_send()
+
+    def weight_8():
         for _, came in w_back_x:
             came.wait_recv()
         w_back_core[0].start()
-
-    def weight_11():
+        for sent, _ in w_back_x:
+            sent.wait_send()
+
+    def weight_9():
         w_back_core[1].wait_recv()
+        w_back_core[0].wait_send()
         for h in range(2):
             for a in range(4):
                 for b in range(4):
@@ -382,6 +400,8 @@
             made.wait()
 
     def compute(c, first, stop):
+        width = CHUNKS[c]
+
         def block(step, acc):
             for inner in range(UNROLL):
                 p = first + step * UNROLL + inner
@@ -390,26 +410,28 @@
                     preferred_element_type=F32,
                 )
                 acc = acc * gate_s[0, p] + product
-                seg[p] = acc.astype(BF16)
+                seg[p, 0:width] = acc.astype(BF16)
             return acc
 
         if first == 0:
-            start = jnp.zeros((T, T), F32)
+            start = jnp.zeros((width, T), F32)
         else:
-            start = acc_ref[...]
+            start = acc_ref[0:width]
         end = lax.fori_loop(0, (stop - first) // UNROLL, block, start)
         if stop < SLOTS:
-            acc_ref[...] = end
+            acc_ref[0:width] = end
 
     def place(c):
+        width = CHUNKS[c]
+
         def one(m, carry):
             major, minor = lax.div(m, 4), lax.rem(m, 4)
-            rows = pl.ds(pl.multiple_of(m * T, T), T)
+            rows = pl.ds(pl.multiple_of(m * width, width), width)
             for dt in range(2):
                 a, b = (major, minor) if dt == 0 else (minor, major)
                 target = (wrap4(x + a) * 4 + wrap4(y + b)) * 2 + dt
-                parts[c, dt, rows] = (
-                    seg[place_s[2, target]].astype(F32) * gate_s[1, target]
+                parts[c][dt, rows] = (
+                    seg[place_s[2, target], 0:width].astype(F32) * gate_s[1, target]
                 ).astype(BF16)
             return carry
 
@@ -420,11 +442,13 @@
         for dt in range(2):
             far = (right_x, left_x) if dt == 0 else (right_y, left_y)
             ring.append(Ring(
-                k, parts.at[c, dt], 256, xl.at[c, dt], xr.at[c, dt], xfl.at[c, dt], xfr.at[c, dt],
-                mids.at[c, dt], *far,
+                k, parts[c].at[dt], 2 * CHUNKS[c],
+                xl[c].at[dt], xr[c].at[dt], xfl[c].at[dt], xfr[c].at[dt], mids[c].at[dt], *far,
             ))
-            fan.append(Fan(k, mids.at[c, dt], T, landed.at[c, dt], all_y if dt == 0 else all_x))
-        cross.append(k.copy(tops.at[c, 1 - depth], ztop.at[c], partner))
+            fan.append(Fan(
+                k, mids[c].at[dt], CHUNKS[c], landed[c].at[dt], all_y if dt == 0 else all_x
+            ))
+        cross.append(k.copy(tops[c].at[1 - depth], ztop[c], partner))
 
     def reduce_1(c):
         for dt in range(2):
@@ -438,102 +462,102 @@
         for dt in range(2):
             ring[2 * c + dt].last()
             fan[2 * c + dt].first()
+        for dt in range(2):
+            ring[2 * c + dt].settle()
 
     def reduce_4(c):
         for dt in range(2):
             fan[2 * c + dt].arrived()
+        width = CHUNKS[c]
         for turn, dt in enumerate((1 - depth, depth)):
-            total = mids[c, dt, 0:T].astype(F32)
+            total = mids[c][dt, 0:width].astype(F32)
             for s in range(3):
-                total = total + landed[c, dt, s * T:(s + 1) * T].astype(F32)
-            tops[c, dt] = total.astype(BF16)
+                total = total + landed[c][dt, s * width:(s + 1) * width].astype(F32)
+            tops[c][dt] = total.astype(BF16)
             if turn == 0:
                 cross[c].start()
+        for dt in range(2):
+            fan[2 * c + dt].settle()
 
     def reduce_5(c):
+        cross[c].wait_send()
         cross[c].wait_recv()
-        node_ref[pl.ds(c * T, T)] = (
-            tops[c, depth].astype(F32) + ztop[c].astype(F32)
+        node_ref[pl.ds(STARTS[c], CHUNKS[c])] = (
+            tops[c][depth].astype(F32) + ztop[c][...].astype(F32)
         ).astype(BF16)
 
     begin(0)
+    sort()
     begin(1)
-    sort()
+    begin(2)
     weight_0()
     forward(0, 1)
-    begin(2)
+    weight_1()
     forward(1, 1)
-    weight_1()
+    forward(2, 1)
     forward(0, 2)
     forward(1, 2)
     begin(3)
-    forward(2, 1)
     weight_2()
+    forward(2, 2)
     forward(0, 3)
+    weight_3()
+    forward(1, 3)
+    forward(3, 1)
+    forward(2, 3)
+    weight_4()
     deliver(0)
-    forward(1, 3)
-    forward(2, 2)
-    forward(3, 1)
+    deliver(1)
+    shared(0)
     loads[4].wait()
-    shared(0)
-
     compute(0, 0, HALF)
-    weight_3()
-    forward(2, 3)
     forward(3, 2)
+    shared(1)
     compute(0, HALF, SLOTS)
+    deliver(2)
     place(0)
     reduce_1(0)
-    deliver(1)
+    compute(1, 0, HALF)
+    shared(2)
     forward(3, 3)
-    shared(1)
-
-    compute(1, 0, HALF)
-    reduce_2(0)
-    weight_4()
     compute(1, HALF, SLOTS)
     place(1)
     reduce_1(1)
-    deliver(2)
-    reduce_3(0)
-    shared(2)
-
     compute(2, 0, HALF)
-    reduce_2(1)
-    weight_5()
-    reduce_4(0)
+    reduce_2(0)
+    deliver(3)
     compute(2, HALF, SLOTS)
     place(2)
     reduce_1(2)
-    deliver(3)
-    reduce_3(1)
-    weight_6()
     shared(3)
-
     compute(3, 0, HALF)
-    reduce_2(2)
-    weight_7()
-    reduce_4(1)
+    reduce_2(1)
+    reduce_3(0)
     compute(3, HALF, SLOTS)
     place(3)
     reduce_1(3)
-
+    reduce_2(2)
+    line_end(0)
+    reduce_3(1)
+    line_end(3)
+    reduce_4(0)
+    line_end(1)
+    line_end(2)
+    weight_5()
+    reduce_2(3)
+    reduce_3(2)
+    reduce_4(1)
+    weight_6()
+    reduce_3(3)
+    reduce_5(0)
+    reduce_4(2)
+    weight_7()
+    reduce_4(3)
+    reduce_5(1)
     weight_8()
-    reduce_3(2)
-    reduce_5(0)
     weight_9()
-    reduce_2(3)
-    reduce_4(2)
-    weight_10()
-    reduce_3(3)
-    reduce_5(1)
-    weight_11()
-    reduce_4(3)
     reduce_5(2)
     reduce_5(3)
-    for made in k.all:
-        made.wait_send()
-    line_end()
 
 
 def on_device(
@@ -543,10 +567,12 @@
     vmem = pl.BlockSpec(memory_space=pltpu.VMEM)
     hbm = pl.BlockSpec(memory_space=pltpu.HBM)
     bf = lambda *shape: pltpu.VMEM(shape, BF16)
+    each = lambda make: tuple(make(width) for width in CHUNKS)
+    two = lambda times: each(lambda width: bf(2, times * width, T))
     node_t, wgrad = pl.pallas_call(
         kernel,
         out_shape=(
-            jax.ShapeDtypeStruct((NCHUNK * T, T), BF16),
+            jax.ShapeDtypeStruct((512, T), BF16),
             jax.ShapeDtypeStruct((512, 512), BF16),
         ),
         in_specs=[smem, vmem, vmem, hbm, hbm, hbm, hbm, hbm],
@@ -554,25 +580,20 @@
         scratch_shapes=[
             bf(T, 512), pltpu.VMEM((T, 512), jnp.int32), bf(T, 512), bf(512, 512),
             bf(SLOTS, T, T), bf(SLOTS, T, T), pltpu.VMEM((T, T), F32),
-            bf(16, T, T), bf(16, T, T), bf(16, T, T), bf(16, T, T),
-            bf(4, 2, 16 * T, T),
-            bf(4, 2, 512, T), bf(4, 2, 512, T), bf(4, 2, 256, T), bf(4, 2, 256, T),
-            bf(4, 2, 512, T),
-            bf(4, 2, 3 * T, T),
-            bf(4, 2, T, T), bf(4, T, T),
-            bf(2, 4, 256, T), bf(4, 256, T), bf(1024, T),
-            bf(256, T), bf(256, T), bf(128, T), bf(128, T),
-            bf(256, T),
-            bf(64, T), bf(64, T), bf(32, T), bf(32, T),
+            each(lambda width: bf(16, width, T)),
+            two(16), two(4), two(4), two(2), two(2), two(4), two(3), two(1),
+            each(lambda width: bf(width, T)),
+            bf(2, 4, 256, T), bf(4, 256, T), bf(1024, T), bf(768, T),
+            bf(256, T), bf(192, T),
             bf(64, T), bf(3, 16, T), bf(4, 16, T), bf(2, 4, 4, 64, T),
             pltpu.VMEM((8, T), jnp.int32), pltpu.VMEM((8, T), jnp.int32), pltpu.VMEM((8, T), F32),
             pltpu.SMEM((8, T), jnp.int32), pltpu.SMEM((8, T), F32),
             pltpu.SemaphoreType.DMA((SEMS,)),
             pltpu.SemaphoreType.DMA((SEMS,)),
-            pltpu.SemaphoreType.DMA((4, 8, 4)),
-            pltpu.SemaphoreType.DMA((4, 8)),
-            pltpu.SemaphoreType.DMA((4, 8)),
-            pltpu.SemaphoreType.DMA((4, 8)),
+            pltpu.SemaphoreType.DMA((NCHUNK, 8, 4)),
+            pltpu.SemaphoreType.DMA((NCHUNK, 8)),
+            pltpu.SemaphoreType.DMA((NCHUNK,)),
+            pltpu.SemaphoreType.DMA((NCHUNK,)),
             pltpu.SemaphoreType.DMA((7,)),
         ],
         compiler_params=pltpu.CompilerParams(

time: 105 us -> 90.1 us (0.86); the launches traced: 104 us -> 89.9 us
  Pallas kernels: 98.4 us -> 84.8 us
    pallas_call x1, Pallas kernels: 98.4 us -> 84.8 us  [on_device(): pl.pallas_call(kernel, out_shape=(jax.ShapeDtypeStruct((512, T), BF16), j...]
where the time goes in v3:
time: 90.1 us; the launch traced here: 89.9 us
  Pallas kernels  84.8 us (94%)
  other arithmetic  2.14 us (2%)
  local copies, waits for them, and re-layouts  1.67 us (2%)
  between operations  1.29 us (1%)
    pallas_call x1, Pallas kernels, on_device(): pl.pallas_call(kernel, out_shape=(jax.ShapeDtypeStruct((512, T), BF16), j...  84.8 us
    convert_element_type x1, other arithmetic, on_device(): return (node_t.T, wgrad.astype(F32))  2.14 us

profile of v3, /device:TPU:1, one launch (start us, length us, event | category | flops | bytes accessed | tf_op | source)
XLA Modules:
  0.0 89.9 jit_solution(1925616929995837335)
XLA Ops:
  1.3 84.8 %shard_map.95 = (bf16[512,128]{1,0:T(8,128)(2,1)}, bf16[512,512]{1,0:T(8,128)(2,1)}) custom-call(s32[1]{0:T(128)S(6)} %copy.11.count_ref, s32[1,84]{1,0:T(1,128)} %bitcast.4, s32[1,84]{1,0:T(1,128)} %bitcast.5, bf16[128,512]{1,0:T(8,128)(2,1)} %grad_hbm.1, s32[128,512]{1,0:T(8,128)} %mask_hbm.1, bf16[128,512]{1,0:T(8,128)(2,1)} %agg_hbm.1, ...), custom_call_target="tpu_custom_call" | custom-call | flops 1600000000 | bytes 5000000 | tf_op jit(solution)/shard_map/pallas_call | solution.py:572
  86.1 1.7 %copy.10 = bf16[128,512]{1,0:T(8,128)(2,1)} copy(bf16[128,512]{0,1:T(8,128)(2,1)} %bitcast.3) | data formatting | bytes 262144
  87.8 2.1 %convert_element_type.3 = f32[512,512]{1,0:T(8,128)} convert(bf16[512,512]{1,0:T(8,128)(2,1)} %get-tuple-element.5) | non-fusion elementwise | flops 262144 | bytes 1572864 | tf_op jit(solution)/shard_map/convert_element_type | solution.py:607

commit v4 on v3

--- a/solution.py
+++ b/solution.py
@@ -560,6 +560,12 @@
     reduce_5(3)
 
 
+def finish(node_t_ref, wgrad_t_ref, node_ref, wgrad_ref):
+    for q in range(4):
+        node_ref[:, q * T:(q + 1) * T] = node_t_ref[q * T:(q + 1) * T].astype(F32).T.astype(BF16)
+    wgrad_ref[...] = wgrad_t_ref[...].astype(F32)
+
+
 def on_device(
     grad_out, relu_mask, aggregated, weight, adjacency_tiles, tile_rows, tile_cols, tile_count
 ):
@@ -604,7 +610,16 @@
         tile_count, tile_rows.reshape(1, SLOTS), tile_cols.reshape(1, SLOTS),
         grad_out, relu_mask, aggregated, weight, adjacency_tiles,
     )
-    return (node_t.T, wgrad.astype(F32))
+    return pl.pallas_call(
+        finish,
+        out_shape=(
+            jax.ShapeDtypeStruct((T, 512), BF16),
+            jax.ShapeDtypeStruct((512, 512), F32),
+        ),
+        in_specs=[vmem, vmem],
+        out_specs=(vmem, vmem),
+        cost_estimate=pl.CostEstimate(flops=300_000, bytes_accessed=1_900_000, transcendentals=0),
+    )(node_t, wgrad)
 
 
 def solution(mesh):

time: 90.1 us -> 88.5 us (0.982)
  Pallas kernels: 84.8 us -> 87 us
  other arithmetic: 2.14 us -> 0 us
  local copies, waits for them, and re-layouts: 1.67 us -> 0 us
    pallas_call x0 -> x1, Pallas kernels: none -> 2.2 us  [on_device(): pl.pallas_call(finish, out_shape=(jax.ShapeDtypeStruct((T, 512), BF16), j...]
    convert_element_type x1 -> x0, other arithmetic: 2.14 us -> none  [on_device(): return (node_t.T, wgrad.astype(F32))]
    unnamed x1 -> x0, local copies, waits for them, and re-layouts: 1.67 us -> none
where the time goes in v4:
time: 88.5 us; the launch traced here: 88.3 us
  Pallas kernels  87 us (98%)
  between operations  1.29 us (1%)
    pallas_call x1, Pallas kernels, on_device(): pl.pallas_call(kernel, out_shape=(jax.ShapeDtypeStruct((512, T), BF16), j...  84.8 us
    pallas_call x1, Pallas kernels, on_device(): pl.pallas_call(finish, out_shape=(jax.ShapeDtypeStruct((T, 512), BF16), j...  2.2 us

profile of v4, /device:TPU:1, one launch (start us, length us, event | category | flops | bytes accessed | tf_op | source)
XLA Modules:
  0.0 88.3 jit_solution(1635767346160855299)
XLA Ops:
  1.3 84.8 %shard_map.95 = (bf16[512,128]{1,0:T(8,128)(2,1)}, bf16[512,512]{1,0:T(8,128)(2,1)}) custom-call(s32[1]{0:T(128)S(6)} %copy.10.count_ref, s32[1,84]{1,0:T(1,128)} %bitcast.2, s32[1,84]{1,0:T(1,128)} %bitcast.3, bf16[128,512]{1,0:T(8,128)(2,1)} %grad_hbm.1, s32[128,512]{1,0:T(8,128)} %mask_hbm.1, bf16[128,512]{1,0:T(8,128)(2,1)} %agg_hbm.1, ...), custom_call_target="tpu_custom_call" | custom-call | flops 1600000000 | bytes 5000000 | tf_op jit(solution)/shard_map/pallas_call | solution.py:578
  86.1 2.2 %shard_map.96 = (bf16[128,512]{1,0:T(8,128)(2,1)}, f32[512,512]{1,0:T(8,128)}) custom-call(bf16[512,128]{1,0:T(8,128)(2,1)} %get-tuple-element.4.node_t_ref, bf16[512,512]{1,0:T(8,128)(2,1)} %get-tuple-element.5.wgrad_t_ref), custom_call_target="tpu_custom_call" | custom-call | flops 300000 | bytes 1900000 | tf_op jit(solution)/shard_map/pallas_call | solution.py:613

commit v5 on v4

--- a/solution.py
+++ b/solution.py
@@ -487,63 +487,63 @@
         ).astype(BF16)
 
     begin(0)
+    begin(1)
     sort()
-    begin(1)
     begin(2)
     weight_0()
     forward(0, 1)
-    weight_1()
     forward(1, 1)
     forward(2, 1)
     forward(0, 2)
     forward(1, 2)
-    begin(3)
-    weight_2()
     forward(2, 2)
     forward(0, 3)
-    weight_3()
+    weight_1()
+    begin(3)
     forward(1, 3)
+    forward(2, 3)
+    deliver(0)
     forward(3, 1)
-    forward(2, 3)
-    weight_4()
-    deliver(0)
-    deliver(1)
+    weight_2()
     shared(0)
     loads[4].wait()
     compute(0, 0, HALF)
+    deliver(1)
+    compute(0, HALF, SLOTS)
+    deliver(2)
     forward(3, 2)
     shared(1)
-    compute(0, HALF, SLOTS)
-    deliver(2)
     place(0)
     reduce_1(0)
     compute(1, 0, HALF)
-    shared(2)
-    forward(3, 3)
     compute(1, HALF, SLOTS)
     place(1)
     reduce_1(1)
+    forward(3, 3)
+    shared(2)
     compute(2, 0, HALF)
     reduce_2(0)
+    weight_3()
+    line_end(2)
+    compute(2, HALF, SLOTS)
     deliver(3)
-    compute(2, HALF, SLOTS)
     place(2)
     reduce_1(2)
+    weight_4()
+    reduce_2(1)
+    reduce_3(0)
     shared(3)
     compute(3, 0, HALF)
-    reduce_2(1)
-    reduce_3(0)
     compute(3, HALF, SLOTS)
     place(3)
     reduce_1(3)
     reduce_2(2)
+    line_end(3)
+    reduce_3(1)
     line_end(0)
-    reduce_3(1)
-    line_end(3)
     reduce_4(0)
+    weight_5()
     line_end(1)
-    line_end(2)
-    weight_5()
     reduce_2(3)
     reduce_3(2)
     reduce_4(1)

time: 88.5 us -> 87 us (0.983)
  Pallas kernels: 87 us -> 85.6 us
    pallas_call x1, Pallas kernels: 84.8 us -> 83.4 us  [on_device(): pl.pallas_call(kernel, out_shape=(jax.ShapeDtypeStruct((512, T), BF16), j...]
where the time goes in v5:
time: 87 us; the launch traced here: 86.8 us
  Pallas kernels  85.6 us (98%)
  between operations  1.29 us (1%)
    pallas_call x1, Pallas kernels, on_device(): pl.pallas_call(kernel, out_shape=(jax.ShapeDtypeStruct((512, T), BF16), j...  83.4 us
    pallas_call x1, Pallas kernels, on_device(): pl.pallas_call(finish, out_shape=(jax.ShapeDtypeStruct((T, 512), BF16), j...  2.2 us

profile of v5, /device:TPU:1, one launch (start us, length us, event | category | flops | bytes accessed | tf_op | source)
XLA Modules:
  0.0 86.8 jit_solution(10890972464444483870)
XLA Ops:
  1.3 83.4 %shard_map.95 = (bf16[512,128]{1,0:T(8,128)(2,1)}, bf16[512,512]{1,0:T(8,128)(2,1)}) custom-call(s32[1]{0:T(128)S(6)} %copy.10.count_ref, s32[1,84]{1,0:T(1,128)} %bitcast.2, s32[1,84]{1,0:T(1,128)} %bitcast.3, bf16[128,512]{1,0:T(8,128)(2,1)} %grad_hbm.1, s32[128,512]{1,0:T(8,128)} %mask_hbm.1, bf16[128,512]{1,0:T(8,128)(2,1)} %agg_hbm.1, ...), custom_call_target="tpu_custom_call" | custom-call | flops 1600000000 | bytes 5000000 | tf_op jit(solution)/shard_map/pallas_call | solution.py:578
  84.6 2.2 %shard_map.96 = (bf16[128,512]{1,0:T(8,128)(2,1)}, f32[512,512]{1,0:T(8,128)}) custom-call(bf16[512,128]{1,0:T(8,128)(2,1)} %get-tuple-element.4.node_t_ref, bf16[512,512]{1,0:T(8,128)(2,1)} %get-tuple-element.5.wgrad_t_ref), custom_call_target="tpu_custom_call" | custom-call | flops 300000 | bytes 1900000 | tf_op jit(solution)/shard_map/pallas_call | solution.py:613

commit v6 on v5

--- a/solution.py
+++ b/solution.py
@@ -14,7 +14,7 @@
 STARTS = tuple(sum(CHUNKS[:c]) for c in range(NCHUNK))
 SLOTS = 84
 GROUP = 32
-UNROLL = 6
+UNROLL = 14
 HALF = SLOTS // 2
 SEMS = 112
 

time: 87 us -> 84.8 us (0.975)
  Pallas kernels: 85.6 us -> 83.3 us
    pallas_call x1, Pallas kernels: 83.4 us -> 81.1 us  [on_device(): pl.pallas_call(kernel, out_shape=(jax.ShapeDtypeStruct((512, T), BF16), j...]
where the time goes in v6:
time: 84.8 us; the launch traced here: 84.6 us
  Pallas kernels  83.3 us (98%)
  between operations  1.29 us (2%)
    pallas_call x1, Pallas kernels, on_device(): pl.pallas_call(kernel, out_shape=(jax.ShapeDtypeStruct((512, T), BF16), j...  81.1 us
    pallas_call x1, Pallas kernels, on_device(): pl.pallas_call(finish, out_shape=(jax.ShapeDtypeStruct((T, 512), BF16), j...  2.2 us

profile of v6, /device:TPU:1, one launch (start us, length us, event | category | flops | bytes accessed | tf_op | source)
XLA Modules:
  0.0 84.6 jit_solution(17755941714382491363)
XLA Ops:
  1.3 81.1 %shard_map.95 = (bf16[512,128]{1,0:T(8,128)(2,1)}, bf16[512,512]{1,0:T(8,128)(2,1)}) custom-call(s32[1]{0:T(128)S(6)} %copy.10.count_ref, s32[1,84]{1,0:T(1,128)} %bitcast.2, s32[1,84]{1,0:T(1,128)} %bitcast.3, bf16[128,512]{1,0:T(8,128)(2,1)} %grad_hbm.1, s32[128,512]{1,0:T(8,128)} %mask_hbm.1, bf16[128,512]{1,0:T(8,128)(2,1)} %agg_hbm.1, ...), custom_call_target="tpu_custom_call" | custom-call | flops 1600000000 | bytes 5000000 | tf_op jit(solution)/shard_map/pallas_call | solution.py:578
  82.4 2.2 %shard_map.96 = (bf16[128,512]{1,0:T(8,128)(2,1)}, f32[512,512]{1,0:T(8,128)}) custom-call(bf16[512,128]{1,0:T(8,128)(2,1)} %get-tuple-element.4.node_t_ref, bf16[512,512]{1,0:T(8,128)(2,1)} %get-tuple-element.5.wgrad_t_ref), custom_call_target="tpu_custom_call" | custom-call | flops 300000 | bytes 1900000 | tf_op jit(solution)/shard_map/pallas_call | solution.py:613
